TPU v7x, 256 devices: a whole 4x4x8 slice. The times are simulated.
256 devices in a mesh: dp: 32 (over z_hi, y, core), own: 8 (over x, z_lo).
Axes of the slice: x: 4, y: 4, z: 8 (z_hi: 4, z_lo: 2; z = z_hi * 2 + z_lo), core: 2. Of those that a mesh axis runs over, the one named last changes fastest.
Arguments:
- activations: bfloat16 [16384, 4096], P('dp', 'own'), may hold values from -40 to 40
- out_grads: bfloat16 [16384, 16384], P('dp', 'own'), may hold values from -40 to 40
- moved_tiles: int32 [32, 8], P('dp', 'own'), may hold values 0 or 1
- stale_roots: bfloat16 [32, 2, 512, 4096], P('dp', None, None, 'own'), may hold values from -7 to 7
Outputs:
- update: bfloat16 [32, 512, 4096], P('dp', None, 'own')
- fresh_roots: bfloat16 [64, 2, 512, 4096], P('dp', None, None, 'own')
All inputs are finite; a program needn't handle non-finite values. No bound on the sum of `moved_tiles` on one device may be relied on, other than what follows from the above.
Results may differ from a plain program's by a relative error of at most 0.025.
Values may be sent and summed in bfloat16 or wider, within the bound.
A program may use at most 128 MiB of HBM per device.

v0:
```python
import jax
import jax.numpy as jnp
from jax import lax
from jax.sharding import PartitionSpec as P

ITERS = 2


EPSILON = 1e-06
POWER = 4.0


def shifted(array, axis, by):
    devices = lax.axis_size(axis)
    return lax.ppermute(array, axis, [(i, (i + by) % devices) for i in range(devices)])


def matmul_high(left_side, right_side):
    return jnp.matmul(left_side, right_side, precision=lax.Precision.HIGHEST)


def refresh_roots(grad_blocks):
    tile_size = grad_blocks.shape[-1]
    left_stat = jnp.einsum(
        "kab,kcb->kac", grad_blocks, grad_blocks, preferred_element_type=jnp.float32
    )
    right_stat = jnp.einsum(
        "kba,kbc->kac", grad_blocks, grad_blocks, preferred_element_type=jnp.float32
    )
    identity = jnp.eye(tile_size, dtype=jnp.float32)
    statistics = jnp.stack([left_stat, right_stat], axis=1) + EPSILON * identity
    frobenius = jnp.sqrt(jnp.sum(statistics * statistics, axis=(2, 3), keepdims=True))
    start_scale = (POWER + 1.0) / (2.0 * frobenius)
    matrix = start_scale * statistics
    inverse_root = jnp.zeros_like(matrix)
    for sweep in range(ITERS):
        factor = ((POWER + 1.0) * identity - matrix) / POWER
        if sweep == 0:
            inverse_root = start_scale ** (1.0 / POWER) * factor
        else:
            inverse_root = matmul_high(inverse_root, factor)
        if sweep + 1 < ITERS:
            squared = matmul_high(factor, factor)
            matrix = matmul_high(matmul_high(squared, squared), matrix)
    return inverse_root.astype(jnp.bfloat16)


def body(activations, out_grads, moved_tiles, stale_roots):
    own_count = lax.axis_size("own")
    dp_count = lax.axis_size("dp")
    per_dev = stale_roots.shape[0]
    tile_size = stale_roots.shape[-1]
    tok_dev = out_grads.shape[0]
    tokens_all = tok_dev * dp_count
    features = lax.all_gather(activations, "own", axis=1, tiled=True)
    row_blocks = features.shape[1] // tile_size
    col_blocks = out_grads.shape[1] // tile_size
    feat_blocks = features.reshape(tok_dev, row_blocks, tile_size)
    grad_columns = out_grads.reshape(tok_dev, col_blocks, tile_size)
    product = jnp.einsum(
        "tra,tcb->rcab", feat_blocks, grad_columns, preferred_element_type=jnp.float32
    )
    product = product.reshape(lax.axis_size("dp") * per_dev, tile_size, tile_size)
    grad_sum = lax.psum_scatter(
        (product / tokens_all).astype(jnp.bfloat16), "dp", scatter_dimension=0, tiled=True
    )
    left_applied = jnp.einsum(
        "kab,kbc->kac", stale_roots[:, 0], grad_sum, preferred_element_type=jnp.float32
    ).astype(jnp.bfloat16)
    precond = jnp.einsum(
        "kab,kbc->kac", left_applied, stale_roots[:, 1], preferred_element_type=jnp.float32
    )
    norm_total = lax.psum(jnp.sum(precond * precond), ("dp", "own"))
    entry_count = per_dev * dp_count * own_count * tile_size * tile_size
    update = (precond * lax.rsqrt(norm_total / entry_count + 1e-06)).astype(jnp.bfloat16)
    move_mask = moved_tiles.astype(jnp.bfloat16).reshape(per_dev, 1, 1, 1)
    keep_mask = jnp.ones_like(move_mask) - move_mask
    arrived_grads, arrived_mask = shifted((grad_sum, move_mask), "dp", 1)
    slot_grads = jnp.concatenate([grad_sum, arrived_grads], axis=0)
    slot_masks = jnp.concatenate([keep_mask, arrived_mask], axis=0)
    fresh_slots = refresh_roots(slot_grads) * slot_masks
    return (update, fresh_slots)


def solution(mesh):
    in_specs = (P("dp", "own"), P("dp", "own"), P("dp", "own"), P("dp", None, None, "own"))
    out_specs = (P("dp", None, "own"), P("dp", None, None, "own"))
    return jax.shard_map(body, mesh=mesh, in_specs=in_specs, out_specs=out_specs, check_vma=False)
```

profile of v0, /device:TPU:1, one launch (start us, length us, event | category | flops | bytes accessed | tf_op | source)
XLA Modules:
  0.0 439.4 jit_solution(11381931186510436594)
XLA Ops:
  7.2 0.0 all-gather.2.cloned.1.call-start
  7.2 2.0 copy.10
  9.3 0.0 all-gather.2.cloned.1.call-update
  9.3 0.0 reduce-scatter.2.cloned.1.call-start
  9.3 2.9 copy.22
  12.2 95.1 %all-gather.2.cloned.1.call-done = bf16[512,4096]{0,1:T(8,128)(2,1)} async-done(((bf16[512,512]{0,1:T(8,128)(2,1)}), bf16[512,4096]{0,1:T(8,128)(2,1)}) %all-gather.2.cloned.1.call-update) | async-done | bytes 4194320 | tf_op jit(solution)/shard_map/all_gather | solution.py:55
  107.3 14.5 %fusion = bf16[8,4,512,512]{2,3,0,1:T(8,128)(2,1)} fusion(bf16[512,4,512,1]{0,2,3,1:T(8,128)(2,1)S(1)} %bitcast.44, bf16[512,8,512,1]{0,2,1,3:T(8,128)(2,1)} %bitcast.45), kind=kOutput, calls=%fused_computation.1 | convolution fusion | flops 8606711808 | bytes 23068672 | tf_op jit(solution)/shard_map/tra,tcb->rcab/dot_general | solution.py:60
  121.8 23.2 %copy.13 = bf16[8,4,512,512]{3,2,1,0:T(8,128)(2,1)} copy(bf16[8,4,512,512]{2,3,0,1:T(8,128)(2,1)} %fusion) | data formatting | bytes 33554432 | tf_op jit(solution)/shard_map/convert_element_type | solution.py:65
  144.9 0.0 reduce-scatter.2.cloned.1.call-update
  145.6 2.8 collective-permute-start.1
  148.5 0.2 fusion.15
  148.7 0.0 collective-permute-done.1
  148.7 0.7 maximum_reduce_fusion
  149.4 162.5 %reduce-scatter.2.cloned.1.call-done = bf16[1,512,512]{2,1,0:T(8,128)(2,1)} async-done(((bf16[32,512,512]{2,1,0:T(8,128)(2,1)}), bf16[1,512,512]{2,1,0:T(8,128)(2,1)}) %reduce-scatter.2.cloned.1.call-update) | async-done | bytes 524304 | tf_op jit(solution)/shard_map/reduce_scatter | solution.py:64
  311.9 2.5 collective-permute-start
  314.4 3.0 multiply_reduce_fusion.1
  317.4 77.0 %psum.7 = f32[]{:T(128)} all-reduce(f32[]{:T(128)} %get-tuple-element.6), channel_id=1, replica_groups=mesh['dp'=32,'own'=8] {'dp','own'}, use_global_device_ids=true, to_apply=%region_2.0 | all-reduce | flops 1 | bytes 8 | tf_op jit(solution)/shard_map/psum | solution.py:73
  395.1 1.1 constant_dynamic-update-slice_fusion.1
  396.2 0.9 fusion.17
  397.1 0.0 collective-permute-done
  397.1 1.1 constant_dynamic-update-slice_fusion
  398.2 0.8 convolution_bitcast_fusion
  398.9 0.7 convolution_bitcast_fusion.1
  399.7 0.7 multiply_reduce_fusion
  400.4 0.9 subtract_multiply_fusion.2
  401.3 7.3 %fusion.3 = f32[2,2,512,512]{3,2,1,0:T(8,128)S(1)} fusion(f32[2,2,512,512]{3,2,0,1:T(8,128)S(1)} %get-tuple-element.5), kind=kOutput, calls=%fused_computation.5 | convolution fusion | flops 6442450944 | bytes 8388608 | tf_op jit(solution)/shard_map/dot_general | solution.py:19
  408.7 7.6 %fusion.30 = f32[2,2,512,512]{3,2,1,0:T(8,128)S(1)} fusion(f32[2,2,512,512]{3,2,1,0:T(8,128)S(1)} %fusion.3), kind=kOutput, calls=%fused_computation.37 | convolution fusion | flops 6442450944 | bytes 8388608 | tf_op jit(solution)/shard_map/dot_general | solution.py:19
  416.3 7.9 %subtract_multiply_fusion = f32[2,2,512,512]{3,2,0,1:T(8,128)S(1)} fusion(f32[2,2]{0,1:T(2,128)S(1)} %get-tuple-element.3, f32[2,2,512,512]{3,2,1,0:T(8,128)S(1)} %fusion.30, f32[512,512]{1,0:T(8,128)S(1)} %get-tuple-element.9, f32[2,1,512,512]{3,2,0,1:T(8,128)S(1)} %convolution_bitcast_fusion, f32[2,1,512,512]{3,2,0,1:T(8,128)S(1)} %convolution_bitcast_fusion.1, ...), kind=kOutput, calls=%fused_computation.10 | convolution fusion | flops 6447693824 | bytes 14680080 | tf_op jit(solution)/shard_map/dot_general | solution.py:19
  424.2 8.3 %convert_multiply_fusion = bf16[2,2,512,512]{3,2,1,0:T(8,128)(2,1)} fusion(bf16[2]{0:T(256)(128)(2,1)S(1)} %maximum_reduce_fusion, f32[2,2,512,512]{3,2,0,1:T(8,128)S(1)} %subtract_multiply_fusion, f32[2,2,512,512]{3,2,0,1:T(8,128)S(1)} %get-tuple-element.4), kind=kOutput, calls=%fused_computation.15 | convolution fusion | flops 6443499520 | bytes 10485764 | tf_op jit(solution)/shard_map/dot_general | solution.py:19
  (1 shorter events, 0.0 us)
Async XLA Ops:
  7.2 100.1 %all-gather.2.cloned.1.call-start = ((), (), s32[]{:S(2)}) async-start(), calls=%async_computation.1 | async-start | bytes 4718592 | tf_op jit(solution)/shard_map/all_gather | solution.py:55
  9.3 302.6 %reduce-scatter.2.cloned.1.call-start = ((), (), s32[]{:S(2)}) async-start(), calls=%async_computation.2 | async-start | bytes 17301504 | tf_op jit(solution)/shard_map/reduce_scatter | solution.py:64
  145.6 3.1 collective-permute-start.1
  311.9 85.2 %collective-permute-start = (bf16[1,512,512]{2,1,0:T(8,128)(2,1)}, bf16[1,512,512]{2,1,0:T(8,128)(2,1)}, u32[]{:S(2)}, u32[]{:S(2)}) collective-permute-start(bf16[1,512,512]{2,1,0:T(8,128)(2,1)} %reduce-scatter.2.cloned.1.call-done), channel_id=1, source_target_pairs={{0,8},{8,16},{16,24},{24,32},{32,40},{40,48},{48,56},{56,64},{64,7... | collective-permute-start | bytes 1572872 | tf_op jit(solution)/shard_map/ppermute | solution.py:15
Sparse Core Ops, SparseCore 0:
  10.4 96.8 all-gather.1
  145.1 166.7 reduce-scatter.1
where the time goes:
time: 440 us; the launch traced here: 439 us
  waiting for transfers between devices  258 us (59%)
  blocking collectives  77 us (18%)
  matrix products  50.2 us (11%)
  local copies, waits for them, and re-layouts  30.2 us (7%)
  between operations  15.5 us (4%)
  starting transfers between devices  5.44 us (1%)
    reduce_scatter x1, waiting for transfers between devices, body(): lax.psum_scatter((product / tokens_all).astype(jnp.bfloat16), 'dp', scatt...  162 us
    all_gather x1, waiting for transfers between devices, body(): features = lax.all_gather(activations, 'own', axis=1, tiled=True)  95.1 us
    psum x1, blocking collectives, body(): norm_total = lax.psum(jnp.sum(precond * precond), ('dp', 'own'))  77 us
    dot_general x4, matrix products, matmul_high(): return jnp.matmul(left_side, right_side, precision=lax.Precision.HIGHEST)  31.2 us
    convert_element_type x1, local copies, waits for them, and re-layouts, body(): (product / tokens_all).astype(jnp.bfloat16)  23.2 us
    dot_general x1, matrix products, body(): jnp.einsum('tra,tcb->rcab', feat_blocks, grad_columns, preferred_element_...  14.5 us
  transfers between devices with their start and end apart: 4, of which 2 were waited for; matrix products, arithmetic and copies ran while one was open for 2% of the time, Pallas kernels for 0%

commit v1 on v0

v1 whole, which is shorter than its diff:
```python
import functools

import jax
import jax.numpy as jnp
from jax import lax
from jax.experimental import pallas as pl
from jax.experimental.pallas import tpu as pltpu
from jax.sharding import PartitionSpec as P

N_DP = 32
N_OWN = 8
BS = 512
HALF = BS // 2
TOKENS = 16384
EPSILON = 1e-06
ENTRIES = N_DP * N_OWN * BS * BS

MESH = pl.DeviceIdType.MESH
F32 = jnp.float32
BF16 = jnp.bfloat16

X_ORDER = (0, 1, 3, 2)
Y_GROUPS = ((0, 1, 0, 512), (1, 1, 0, 512)) + tuple((2, 2, 128 * s, 128) for s in range(4))
Z_GROUPS = tuple((128 * s, 128) for s in range(4))

N_SEMS = 19 + 2 + 1 + len(Y_GROUPS) * 6 + len(Z_GROUPS) * 7 + 17


def dot(left, right, contract=(1, 0)):
    dims = (((contract[0],), (contract[1],)), ((), ()))
    return lax.dot_general(left, right, dims, preferred_element_type=F32)


def identity_rows(first_row, rows):
    row = lax.broadcasted_iota(jnp.int32, (rows, BS), 0) + first_row
    column = lax.broadcasted_iota(jnp.int32, (rows, BS), 1)
    return (row == column).astype(F32)


def kernel(
    act, grads, moved, stale,
    update, fresh,
    act_own, a_all, b_all, part,
    y_relay_lo, y_relay_hi, y_sum_lo, y_sum_hi, y_from_minus, y_from_plus,
    ysum,
    z_relay_lo, z_relay_hi, z_sum_lo, z_sum_hi, z_from_minus, z_from_plus,
    grad, grad_prev, flag, flag_prev, stale_v,
    left_applied, precond, stat, stat_b, mid_n, mid_e, mid_t, mid_tb,
    norm1, norm2, norm3,
    send_sems, recv_sems, local_sems,
):
    dp = lax.axis_index("dp")
    own = lax.axis_index("own")
    core = lax.rem(dp, 2)
    y = lax.rem(dp // 2, 4)
    z = dp // 8
    x = own // 2
    z_lo = lax.rem(own, 2)

    sibling = dp + 1 - 2 * core
    pair = own + 1 - 2 * z_lo
    x_plus, x_minus = lax.rem(own + 2, N_OWN), lax.rem(own + 6, N_OWN)

    def dp_y(by):
        return z * 8 + lax.rem(y + by, 4) * 2 + core

    def dp_low(by):
        return z * 8 + lax.rem(lax.rem(dp, 8) + by, 8)

    def dp_z(by):
        return lax.rem(dp + 8 * by, N_DP)

    def own_at(by):
        return lax.rem(own + by, N_OWN)

    sent = []
    counter = [0]

    def new_sem():
        counter[0] += 1
        return counter[0] - 1

    def send(n, src, dst, to_dp, to_own):
        copy = pltpu.make_async_remote_copy(
            src_ref=src, dst_ref=dst, send_sem=send_sems.at[n], recv_sem=recv_sems.at[n],
            device_id=(to_dp, to_own), device_id_type=MESH,
        )
        copy.start()
        sent.append(copy)

    def arrive(n, dst):
        pltpu.make_async_remote_copy(
            src_ref=dst, dst_ref=dst, send_sem=send_sems.at[n], recv_sem=recv_sems.at[n],
            device_id=(sibling, own), device_id_type=MESH,
        ).wait_recv()

    load_act = pltpu.make_async_copy(act, act_own, local_sems.at[0])
    load_act.start()
    load_b = []
    for ch in range(2):
        load = pltpu.make_async_copy(
            grads.at[:, pl.ds(pl.multiple_of((2 * ch + core) * BS, BS), BS)],
            b_all.at[ch, pl.ds(pl.multiple_of(core * BS, BS), BS), :],
            local_sems.at[1 + ch],
        )
        load.start()
        load_b.append(load)
    load_stale = pltpu.make_async_copy(stale, stale_v, local_sems.at[3])
    load_stale.start()

    cross = lax.rem(dp + 2 * core - 1 + N_DP, N_DP)
    barrier = pltpu.get_barrier_semaphore()
    partners = [(dp, own_at(i)) for i in range(1, 8)]
    partners += [(dp_low(i), own) for i in range(1, 8)]
    partners += [(dp_z(i), own) for i in range(1, 4)]
    partners += [(cross, own)]
    for partner in partners:
        pl.semaphore_signal(barrier, inc=1, device_id=partner, device_id_type=MESH)

    my_tokens = pl.ds(pl.multiple_of(core * BS, BS), BS)
    sib_tokens = pl.ds(pl.multiple_of((1 - core) * BS, BS), BS)
    load_act.wait()
    for i in range(4):
        a_all[own, i * 128:(i + 1) * 128, my_tokens] = act_own[:, i * 128:(i + 1) * 128].T
    flag[...] = jnp.full((8, 128), moved[0, 0].astype(F32))

    pl.semaphore_wait(barrier, len(partners))

    def block(r, tokens, half=None):
        if half is None:
            return a_all.at[r, :, tokens]
        return a_all.at[r, half * HALF:(half + 1) * HALF, tokens]

    n_flag = new_sem()
    n_b = [new_sem() for _ in range(2)]
    n_sib = {}

    def to_sibling(key, r, half=None):
        n_sib[key] = new_sem()
        send(n_sib[key], block(r, my_tokens, half), block(r, my_tokens, half), sibling, own)

    def from_sibling(key, r, half=None):
        arrive(n_sib[key], block(r, sib_tokens, half))

    n_pair = new_sem()
    send(n_pair, block(own, my_tokens), block(own, my_tokens), dp, pair)
    to_sibling("own", own)
    n_xp, n_xm = new_sem(), new_sem()
    send(n_xp, block(own, my_tokens), block(own, my_tokens), dp, x_plus)
    send(n_xm, block(own, my_tokens), block(own, my_tokens), dp, x_minus)
    for ch in range(2):
        send(
            n_b[ch],
            grads.at[:, pl.ds(pl.multiple_of((2 * ch + 1 - core) * BS, BS), BS)],
            b_all.at[ch, my_tokens, :],
            sibling, own,
        )
    next_dp = lax.rem(dp + 1, N_DP)
    send(n_flag, flag, flag_prev, next_dp, own)

    def products(r, slot):
        @pl.loop(0, 4)
        def _(i):
            ch = i // 2
            rows = pl.ds(pl.multiple_of(lax.rem(i, 2) * HALF, HALF), HALF)
            value = dot(a_all[r, rows, :], b_all[ch]) * (1.0 / TOKENS)
            target = lax.rem(lax.rem(r, 2) * 2 + ch - y + 4, 4)
            part[slot, target, rows, :] = value.astype(BF16)

    for load in load_b:
        load.wait()
    for ch in range(2):
        arrive(n_b[ch], b_all.at[ch, sib_tokens, :])
    from_sibling("own", own)
    products(own, 0)

    def tree_a(src, relay_lo, relay_hi, from_minus, from_plus, to_plus, to_minus, sems):
        send(sems[0], src(2, 0), relay_lo, *to_plus)
        send(sems[1], src(2, 1), relay_hi, *to_minus)
        send(sems[2], src(1, 1), from_minus(1), *to_plus)
        send(sems[3], src(3, 0), from_plus(0), *to_minus)

    def y_views(group):
        first, many, column, columns = Y_GROUPS[group]
        cols = slice(column, column + columns)
        slots = slice(first, first + many)

        def src(rho, half):
            return part.at[slots, rho, half * HALF:(half + 1) * HALF, cols]

        def half_of(ref):
            return lambda half: ref.at[slots, half * HALF:(half + 1) * HALF, cols]

        def piece(ref):
            return ref.at[slots, :, cols]

        return src, half_of, piece

    y_sems = [[new_sem() for _ in range(6)] for _ in Y_GROUPS]
    z_sems = [[new_sem() for _ in range(6)] for _ in Z_GROUPS]
    to_y = ((dp_y(1), own), (dp_y(3), own))
    to_z = ((dp_z(1), own), (dp_z(3), own))

    def y_a(group):
        src, half_of, piece = y_views(group)
        tree_a(src, piece(y_relay_lo), piece(y_relay_hi), half_of(y_from_minus),
               half_of(y_from_plus), *to_y, y_sems[group])

    def y_b(group):
        src, half_of, piece = y_views(group)
        sems = y_sems[group]
        arrive(sems[0], piece(y_relay_lo))
        piece(y_sum_lo)[...] = src(1, 0)[...] + piece(y_relay_lo)[...]
        send(sems[4], piece(y_sum_lo), half_of(y_from_minus)(0), *to_y[0])
        arrive(sems[1], piece(y_relay_hi))
        piece(y_sum_hi)[...] = src(3, 1)[...] + piece(y_relay_hi)[...]
        send(sems[5], piece(y_sum_hi), half_of(y_from_plus)(1), *to_y[1])

    def y_c(group):
        src, half_of, piece = y_views(group)
        sems = y_sems[group]
        arrive(sems[2], half_of(y_from_minus)(1))
        arrive(sems[3], half_of(y_from_plus)(0))
        arrive(sems[4], half_of(y_from_minus)(0))
        arrive(sems[5], half_of(y_from_plus)(1))
        first, many, column, columns = Y_GROUPS[group]
        cols = slice(column, column + columns)
        for slot in range(first, first + many):
            target = lax.rem(x + X_ORDER[slot] - z + 4, 4)
            total = part[slot, 0, :, cols].astype(F32) + y_from_minus[slot, :, cols].astype(F32)
            total = total + y_from_plus[slot, :, cols].astype(F32)
            ysum[target, :, cols] = total.astype(BF16)

    def z_views(group):
        column, columns = Z_GROUPS[group]
        cols = slice(column, column + columns)

        def src(rho, half):
            return ysum.at[rho, half * HALF:(half + 1) * HALF, cols]

        def half_of(ref):
            return lambda half: ref.at[half * HALF:(half + 1) * HALF, cols]

        def piece(ref):
            return ref.at[:, cols]

        return src, half_of, piece

    def z_a(group):
        src, half_of, piece = z_views(group)
        tree_a(src, piece(z_relay_lo), piece(z_relay_hi), half_of(z_from_minus),
               half_of(z_from_plus), *to_z, z_sems[group])

    def z_b(group):
        src, half_of, piece = z_views(group)
        sems = z_sems[group]
        arrive(sems[0], piece(z_relay_lo))
        piece(z_sum_lo)[...] = src(1, 0)[...] + piece(z_relay_lo)[...]
        send(sems[4], piece(z_sum_lo), half_of(z_from_minus)(0), *to_z[0])
        arrive(sems[1], piece(z_relay_hi))
        piece(z_sum_hi)[...] = src(3, 1)[...] + piece(z_relay_hi)[...]
        send(sems[5], piece(z_sum_hi), half_of(z_from_plus)(1), *to_z[1])

    grad_sems = [new_sem() for _ in Z_GROUPS]

    def z_c(group):
        src, half_of, piece = z_views(group)
        sems = z_sems[group]
        arrive(sems[2], half_of(z_from_minus)(1))
        arrive(sems[3], half_of(z_from_plus)(0))
        arrive(sems[4], half_of(z_from_minus)(0))
        arrive(sems[5], half_of(z_from_plus)(1))
        column, columns = Z_GROUPS[group]
        cols = slice(column, column + columns)
        total = ysum[0, :, cols].astype(F32) + z_from_minus[:, cols].astype(F32)
        total = total + z_from_plus[:, cols].astype(F32)
        grad[:, cols] = total.astype(BF16)
        send(grad_sems[group], grad.at[:, cols], grad_prev.at[:, cols], next_dp, own)

    arrive(n_pair, block(pair, my_tokens))
    to_sibling("pair", pair)
    n_xp2, n_xm2 = new_sem(), new_sem()
    send(n_xp2, block(pair, my_tokens), block(pair, my_tokens), dp, x_plus)
    send(n_xm2, block(pair, my_tokens), block(pair, my_tokens), dp, x_minus)
    from_sibling("pair", pair)
    products(pair, 0)
    y_a(0)

    pair_plus, pair_minus = lax.rem(pair + 2, N_OWN), lax.rem(pair + 6, N_OWN)
    far, pair_far = lax.rem(own + 4, N_OWN), lax.rem(pair + 4, N_OWN)
    arrive(n_xp, block(x_minus, my_tokens))
    to_sibling("minus", x_minus)
    n_far = {}
    n_far["own", 0] = new_sem()
    send(n_far["own", 0], block(x_minus, my_tokens, 0), block(x_minus, my_tokens, 0), dp, x_plus)
    arrive(n_xm, block(x_plus, my_tokens))
    to_sibling("plus", x_plus)
    n_far["own", 1] = new_sem()
    send(n_far["own", 1], block(x_plus, my_tokens, 1), block(x_plus, my_tokens, 1), dp, x_minus)
    from_sibling("plus", x_plus)
    products(x_plus, 1)
    from_sibling("minus", x_minus)
    products(x_minus, 2)
    y_b(0)

    arrive(n_xm2, block(pair_plus, my_tokens))
    to_sibling("pair_plus", pair_plus)
    n_far["pair", 1] = new_sem()
    send(n_far["pair", 1], block(pair_plus, my_tokens, 1), block(pair_plus, my_tokens, 1), dp, x_minus)
    arrive(n_xp2, block(pair_minus, my_tokens))
    to_sibling("pair_minus", pair_minus)
    n_far["pair", 0] = new_sem()
    send(n_far["pair", 0], block(pair_minus, my_tokens, 0), block(pair_minus, my_tokens, 0), dp, x_plus)
    from_sibling("pair_plus", pair_plus)
    products(pair_plus, 1)
    y_a(1)
    from_sibling("pair_minus", pair_minus)
    products(pair_minus, 2)
    y_c(0)

    for name, r in (("own", far), ("pair", pair_far)):
        for half in range(2):
            arrive(n_far[name, half], block(r, my_tokens, half))
            to_sibling(("far", name, half), r, half)
    y_b(1)
    for name, r in (("own", far), ("pair", pair_far)):
        for half in range(2):
            from_sibling(("far", name, half), r, half)
        products(r, 3)

    y_a(2)
    y_c(1)
    y_b(2)
    y_a(3)
    y_c(2)
    z_a(0)
    y_b(3)
    y_a(4)
    z_b(0)
    y_c(3)
    z_a(1)
    y_b(4)
    y_a(5)
    z_c(0)
    z_b(1)
    y_c(4)
    z_a(2)
    y_b(5)
    z_c(1)
    z_b(2)
    y_c(5)
    z_a(3)
    z_c(2)
    z_b(3)
    z_c(3)

    load_stale.wait()
    squares = jnp.zeros((1, 1), F32)
    for half in range(2):
        rows = slice(half * HALF, (half + 1) * HALF)
        left_applied[rows, :] = dot(stale_v[0, 0, rows, :], grad[...]).astype(BF16)
        value = dot(left_applied[rows, :], stale_v[0, 1])
        precond[rows, :] = value
        squares = squares + jnp.sum(value * value, keepdims=True)

    def spread(store, value, targets):
        store[0] = jnp.broadcast_to(value, (8, 128))
        sems = [new_sem() for _ in targets]
        for i, target in enumerate(targets):
            send(sems[i], store.at[0], store.at[i + 1], *target)
        return sems

    def collect(store, sems):
        for i, n in enumerate(sems):
            arrive(n, store.at[i + 1])
        return jnp.sum(store[...], axis=0)[0:1, 0:1]

    def root(tile, side, slot, keep):
        total = jnp.zeros((1, 1), F32)
        for half in range(2):
            rows = slice(half * HALF, (half + 1) * HALF)
            if side == 0:
                value = dot(tile[rows, :], tile[...], (1, 1))
            else:
                value = dot(tile[:, rows], tile[...], (0, 0))
            value = value + EPSILON * identity_rows(half * HALF, HALF)
            stat[rows, :] = value
            total = total + jnp.sum(value * value, keepdims=True)
        scale = 2.5 / jnp.sqrt(total)
        matrix = stat[...] * scale
        stat[...] = matrix
        stat_b[...] = matrix.astype(BF16)
        for half in range(2):
            rows = slice(half * HALF, (half + 1) * HALF)
            squared = dot(stat_b[rows, :], stat_b[...])
            matrix = stat[rows, :]
            mid_n[rows, :] = (5.0 * matrix - squared) * 0.25
            mid_e[rows, :] = ((squared - 10.0 * matrix) * 0.0625).astype(BF16)
        for half in range(2):
            rows = slice(half * HALF, (half + 1) * HALF)
            value = 1.5625 * mid_n[rows, :] + dot(mid_e[rows, :], mid_n[...].astype(BF16))
            mid_t[rows, :] = value
            mid_tb[rows, :] = value.astype(BF16)
        factor = jnp.sqrt(jnp.sqrt(scale)) * 0.25
        for half in range(2):
            rows = slice(half * HALF, (half + 1) * HALF)
            value = 1.5625 * mid_t[rows, :] + dot(mid_e[rows, :], mid_tb[...])
            first = (25.0 * identity_rows(half * HALF, HALF) - 5.0 * stat[rows, :]) * 0.25
            result = ((first - value) * factor).astype(BF16)
            fresh[slot, side, rows, :] = (result.astype(F32) * keep).astype(BF16)

    sems1 = spread(norm1, squares, [(dp, own_at(i)) for i in range(1, 8)])
    keep = 1.0 - flag[0:1, 0:1]
    root(grad, 0, 0, keep)
    sems2 = spread(norm2, collect(norm1, sems1), [(dp_low(i), own) for i in range(1, 8)])
    root(grad, 1, 0, keep)
    sems3 = spread(norm3, collect(norm2, sems2), [(dp_z(i), own) for i in range(1, 4)])
    arrive(n_flag, flag_prev)
    for group, (column, columns) in enumerate(Z_GROUPS):
        arrive(grad_sems[group], grad_prev.at[:, column:column + columns])
    keep = flag_prev[0:1, 0:1]
    root(grad_prev, 0, 1, keep)
    norm_total = collect(norm3, sems3)
    update[0] = (precond[...] * lax.rsqrt(norm_total / ENTRIES + 1e-06)).astype(BF16)
    root(grad_prev, 1, 1, keep)

    for copy in sent:
        copy.wait_send()
    assert counter[0] <= N_SEMS, counter[0]


def body(activations, out_grads, moved_tiles, stale_roots):
    tile = (BS, BS)
    half = (HALF, BS)
    scratch = [
        ((BS, BS), BF16),
        ((N_OWN, BS, 2 * BS), BF16),
        ((2, 2 * BS, BS), BF16),
        ((4, 4) + tile, BF16),
        ((4,) + half, BF16), ((4,) + half, BF16), ((4,) + half, BF16), ((4,) + half, BF16),
        ((4,) + tile, BF16), ((4,) + tile, BF16),
        ((4,) + tile, BF16),
        (half, BF16), (half, BF16), (half, BF16), (half, BF16), (tile, BF16), (tile, BF16),
        (tile, BF16), (tile, BF16), ((8, 128), F32), ((8, 128), F32), ((1, 2) + tile, BF16),
        (tile, BF16), (tile, F32), (tile, F32), (tile, BF16), (tile, F32), (tile, BF16),
        (tile, F32), (tile, BF16),
        ((8, 8, 128), F32), ((8, 8, 128), F32), ((4, 8, 128), F32),
    ]
    flops = 2 * 2 * 512 * 4096 * 2048
    return tuple(pl.pallas_call(
        kernel,
        out_shape=(
            jax.ShapeDtypeStruct((1, BS, BS), BF16),
            jax.ShapeDtypeStruct((2, 2, BS, BS), BF16),
        ),
        in_specs=[
            pl.BlockSpec(memory_space=pl.ANY),
            pl.BlockSpec(memory_space=pl.ANY),
            pl.BlockSpec(memory_space=pltpu.SMEM),
            pl.BlockSpec(memory_space=pl.ANY),
        ],
        out_specs=(pl.BlockSpec(memory_space=pltpu.VMEM), pl.BlockSpec(memory_space=pltpu.VMEM)),
        scratch_shapes=[pltpu.VMEM(shape, dtype) for shape, dtype in scratch] + [
            pltpu.SemaphoreType.DMA((N_SEMS,)),
            pltpu.SemaphoreType.DMA((N_SEMS,)),
            pltpu.SemaphoreType.DMA((4,)),
        ],
        compiler_params=pltpu.CompilerParams(
            collective_id=0, has_side_effects=True, vmem_limit_bytes=60 * 1024 * 1024
        ),
        cost_estimate=pl.CostEstimate(flops=flops, bytes_accessed=6 << 20, transcendentals=0),
    )(activations, out_grads, moved_tiles, stale_roots))


def solution(mesh):
    in_specs = (P("dp", "own"), P("dp", "own"), P("dp", "own"), P("dp", None, None, "own"))
    out_specs = (P("dp", None, "own"), P("dp", None, None, "own"))
    return jax.shard_map(body, mesh=mesh, in_specs=in_specs, out_specs=out_specs, check_vma=False)
```

time: 440 us -> 140 us (0.32)
  waiting for transfers between devices: 258 us -> 0 us
  Pallas kernels: 0 us -> 134 us
  blocking collectives: 77 us -> 0 us
  matrix products: 50.2 us -> 0 us
  local copies, waits for them, and re-layouts: 30.2 us -> 4.91 us
  between operations: 15.5 us -> 1.29 us
  starting transfers between devices: 5.44 us -> 0 us
    reduce_scatter x1 -> x0, waiting for transfers between devices: 162 us -> none  [body(): lax.psum_scatter((product / tokens_all).astype(jnp.bfloat16), 'dp', scatt...]
    pallas_call x0 -> x1, Pallas kernels: none -> 134 us  [body(): pl.pallas_call(kernel, out_shape=(jax.ShapeDtypeStruct((1, BS, BS), BF16)...]
    all_gather x1 -> x0, waiting for transfers between devices: 95.1 us -> none  [body(): features = lax.all_gather(activations, 'own', axis=1, tiled=True)]
    psum x1 -> x0, blocking collectives: 77 us -> none  [body(): norm_total = lax.psum(jnp.sum(precond * precond), ('dp', 'own'))]
    dot_general x8 -> x0, matrix products: 50.2 us -> none  [the longest x4 31.2 us: matmul_high(): return jnp.matmul(left_side, right_side, precision=lax.Precision.HIGHEST)]
    convert_element_type x1 -> x0, local copies, waits for them, and re-layouts: 23.2 us -> none  [body(): (product / tokens_all).astype(jnp.bfloat16)]
    ppermute x2 -> x0, starting transfers between devices: 5.36 us -> none  [shifted(): lax.ppermute(array, axis, [(i, (i + by) % devices) for i in range(devices)])]
  transfers between devices with their start and end apart: 4 -> 0, of which waited for: 2 -> 0; matrix products, arithmetic and copies ran while one was open for 2% -> 0% of each run, Pallas kernels for 0% -> 0%
where the time goes in v1:
time: 140 us
  Pallas kernels  134 us (96%)
  local copies, waits for them, and re-layouts  4.91 us (4%)
    pallas_call x1, Pallas kernels, body(): pl.pallas_call(kernel, out_shape=(jax.ShapeDtypeStruct((1, BS, BS), BF16)...  134 us
    unnamed x2, local copies, waits for them, and re-layouts  4.91 us

profile of v1, /device:TPU:1, one launch (start us, length us, event | category | flops | bytes accessed | tf_op | source)
XLA Modules:
  0.0 139.8 jit_solution(13672543467129118563)
XLA Ops:
  1.3 133.6 %shard_map.59 = (bf16[1,512,512]{2,1,0:T(8,128)(2,1)}, bf16[2,2,512,512]{3,2,1,0:T(8,128)(2,1)}) custom-call(bf16[512,512]{1,0:T(8,128)(2,1)} %act.1, bf16[512,2048]{1,0:T(8,128)(2,1)} %grads.1, s32[1,1]{1,0:T(1,128)S(6)} %copy.8.moved, bf16[1,2,512,512]{3,2,1,0:T(8,128)(2,1)} %stale.1), custom_call_target="tpu_custom_call" | custom-call | flops 17179869184 | bytes 6291456 | tf_op jit(solution)/shard_map/pallas_call | solution.py:450
  134.9 1.9 %copy.9 = bf16[1,512,512]{2,1,0:T(8,128)(2,1)} copy(bf16[1,512,512]{2,1,0:T(8,128)(2,1)} %get-tuple-element.4) | data formatting | bytes 1048576
  136.8 3.0 %copy.10 = bf16[2,2,512,512]{3,2,1,0:T(8,128)(2,1)} copy(bf16[2,2,512,512]{3,2,1,0:T(8,128)(2,1)} %get-tuple-element.5) | data formatting | bytes 4194304

commit v2 on v1

v2 whole, which is shorter than its diff:
```python
import functools

import jax
import jax.numpy as jnp
from jax import lax
from jax.experimental import pallas as pl
from jax.experimental.pallas import tpu as pltpu
from jax.sharding import PartitionSpec as P

N_DP = 32
N_OWN = 8
BS = 512
HALF = BS // 2
TOKENS = 16384
EPSILON = 1e-06
ENTRIES = N_DP * N_OWN * BS * BS

MESH = pl.DeviceIdType.MESH
F32 = jnp.float32
BF16 = jnp.bfloat16

X_ORDER = (0, 1, 3, 2)
SLICE = 128
SLICES = BS // SLICE
Y_PIECES = (
    (0, 1, 0, 128), (0, 1, 128, 128), (0, 1, 256, 128), (0, 1, 384, 128), (1, 3, 0, 128),
    (3, 4, 0, 128), (1, 4, 128, 64), (1, 4, 192, 64), (1, 4, 256, 64), (1, 4, 320, 64),
    (1, 4, 384, 64), (1, 4, 448, 64),
)
Z_PIECES = ((0, 64), (64, 64), (128, 64), (192, 64), (256, 64), (320, 64), (384, 64), (448, 64))

N_SEMS = 320


def dot(left, right, contract=(1, 0)):
    dims = (((contract[0],), (contract[1],)), ((), ()))
    return lax.dot_general(left, right, dims, preferred_element_type=F32)


def identity_rows(first_row, rows):
    row = lax.broadcasted_iota(jnp.int32, (rows, BS), 0) + first_row
    column = lax.broadcasted_iota(jnp.int32, (rows, BS), 1)
    return (row == column).astype(F32)


def kernel(
    act, grads, moved, stale,
    precond_out, fresh_out, norm_out,
    a_all, b_all, part,
    y_relay, y_sum, y_from_minus, y_from_plus,
    ysum,
    z_relay, z_sum, z_from_minus, z_from_plus,
    grad, grad_prev, flag, flag_prev, stale_v,
    left_applied, precond, stat, stat_b, mid_n, mid_e, mid_t, mid_tb,
    norm1, norm2, fresh,
    send_sems, recv_sems, local_sems,
):
    dp = lax.axis_index("dp")
    own = lax.axis_index("own")
    core = lax.rem(dp, 2)
    y = lax.rem(dp // 2, 4)
    z = dp // 8
    x = own // 2
    z_lo = lax.rem(own, 2)

    sibling = dp + 1 - 2 * core
    pair = own + 1 - 2 * z_lo
    x_plus, x_minus = lax.rem(own + 2, N_OWN), lax.rem(own + 6, N_OWN)

    def dp_y(by):
        return z * 8 + lax.rem(y + by, 4) * 2 + core

    def dp_at(by):
        return lax.rem(dp + by, N_DP)

    def dp_z(by):
        return dp_at(8 * by)

    def own_at(by):
        return lax.rem(own + by, N_OWN)

    sent = []
    counter = [0]
    my_tokens = pl.ds(pl.multiple_of(core * BS, BS), BS)
    sib_tokens = pl.ds(pl.multiple_of((1 - core) * BS, BS), BS)

    def new_sem():
        counter[0] += 1
        return counter[0] - 1

    def send(n, src, dst, to_dp, to_own, keep=True):
        copy = pltpu.make_async_remote_copy(
            src_ref=src, dst_ref=dst, send_sem=send_sems.at[n], recv_sem=recv_sems.at[n],
            device_id=(to_dp, to_own), device_id_type=MESH,
        )
        copy.start()
        if keep:
            sent.append((n, src.shape))

    def arrive(n, dst):
        pltpu.make_async_remote_copy(
            src_ref=dst, dst_ref=dst, send_sem=send_sems.at[n], recv_sem=recv_sems.at[n],
            device_id=(sibling, own), device_id_type=MESH,
        ).wait_recv()

    def features(part_of):
        return slice(part_of * SLICE, (part_of + 1) * SLICE)

    def block(r, part_of, tokens):
        return a_all.at[part_of, tokens, pl.ds(pl.multiple_of(r * SLICE, SLICE), SLICE)]

    def slab(at_x, part_of, tokens):
        return a_all.at[part_of, tokens, pl.ds(pl.multiple_of(at_x * 2 * SLICE, 2 * SLICE), 2 * SLICE)]

    def half_of(tokens, half):
        return pl.ds(pl.multiple_of(tokens.start + half * HALF, HALF), HALF)

    load_act = []
    for part_of in range(SLICES):
        load = pltpu.make_async_copy(act.at[:, features(part_of)], block(own, part_of, my_tokens), local_sems.at[4 + part_of])
        load.start()
        load_act.append(load)
    load_b = []
    for ch in range(2):
        load = pltpu.make_async_copy(
            grads.at[:, pl.ds(pl.multiple_of((2 * ch + core) * BS, BS), BS)],
            b_all.at[ch, pl.ds(pl.multiple_of(core * BS, BS), BS), :],
            local_sems.at[1 + ch],
        )
        load.start()
        load_b.append(load)
    load_stale = pltpu.make_async_copy(stale, stale_v, local_sems.at[3])
    load_stale.start()

    barrier = pltpu.get_barrier_semaphore()
    partners = [(dp, own_at(i)) for i in range(1, 8)]
    partners += [(dp_at(i), own) for i in range(1, N_DP)]
    for partner in partners:
        pl.semaphore_signal(barrier, inc=1, device_id=partner, device_id_type=MESH)

    flag[...] = jnp.full((8, 128), moved[0, 0].astype(F32))

    pl.semaphore_wait(barrier, len(partners))

    n_flag = new_sem()
    n_b = [new_sem() for _ in range(2)]
    n_own = [new_sem() for _ in range(SLICES)]
    n_pair = [new_sem() for _ in range(SLICES)]
    next_dp = lax.rem(dp + 1, N_DP)
    for ch in range(2):
        send(
            n_b[ch],
            grads.at[:, pl.ds(pl.multiple_of((2 * ch + 1 - core) * BS, BS), BS)],
            b_all.at[ch, my_tokens, :],
            sibling, own,
        )
    n_first_up, n_first_down = new_sem(), new_sem()
    for part_of in range(SLICES):
        target = block(own, part_of, my_tokens)
        send(n_pair[part_of], act.at[:, features(part_of)], target, dp, pair)
        send(n_own[part_of], act.at[:, features(part_of)], target, sibling, own)
        if part_of == 0:
            send(n_first_up, act.at[:, features(0)], target, dp, x_plus)
            send(n_first_down, act.at[:, features(0)], target, dp, x_minus)
    send(n_flag, flag, flag_prev, next_dp, own)

    def products_here(r, part_of):
        for ch in range(2):
            target = lax.rem(lax.rem(r, 2) * 2 + ch - y + 4, 4)
            lanes = pl.ds(pl.multiple_of(r * SLICE, SLICE), SLICE)
            value = dot(a_all[part_of, :, lanes], b_all[ch], (0, 0)) * (1.0 / TOKENS)
            part[0, target, features(part_of), :] = value.astype(BF16)

    def products(part_of, first, last):
        rows = features(part_of)
        for ch in range(2):
            @pl.loop(first, last)
            def _(slot):
                at_x = lax.rem(x + slot + slot // 2 - 2 * (slot // 3), 4)
                lanes = pl.ds(pl.multiple_of(at_x * 2 * SLICE, 2 * SLICE), 2 * SLICE)
                value = dot(a_all[part_of, :, lanes], b_all[ch], (0, 0)) * (1.0 / TOKENS)
                value = value.astype(BF16)
                for parity in range(2):
                    target = lax.rem(2 * parity + ch - y + 4, 4)
                    part[slot, target, rows, :] = value[parity * SLICE:(parity + 1) * SLICE]

    for load in load_act + load_b:
        load.wait()
    for ch in range(2):
        arrive(n_b[ch], b_all.at[ch, sib_tokens, :])
    y_sems = [[new_sem() for _ in range(6)] for _ in Y_PIECES]
    z_sems = [[new_sem() for _ in range(6)] for _ in Z_PIECES]
    grad_sems = [new_sem() for _ in Z_PIECES]
    y_up, y_down = (dp_y(1), own), (dp_y(3), own)
    z_up, z_down = (dp_z(1), own), (dp_z(3), own)

    def cut(first, rows):
        middle = first + rows // 2
        return slice(first, middle), slice(middle, first + rows)

    in_first = [lax.rem(y + by, 4) // 2 == z_lo for by in range(4)]

    def y_far(piece, keep=True):
        start, stop, row, rows = Y_PIECES[piece]
        lo, hi = cut(row, rows)
        sems = y_sems[piece]
        send(sems[0], part.at[start:stop, 2, lo], y_relay.at[start:stop, lo], *y_up, keep=keep)
        send(sems[1], part.at[start:stop, 2, hi], y_relay.at[start:stop, hi], *y_down, keep=keep)

    def y_near(piece, by, keep=True):
        start, stop, row, rows = Y_PIECES[piece]
        lo, hi = cut(row, rows)
        sems = y_sems[piece]
        if by == 1:
            send(sems[2], part.at[start:stop, 1, hi], y_from_minus.at[start:stop, hi], *y_up, keep=keep)
        else:
            send(sems[3], part.at[start:stop, 3, lo], y_from_plus.at[start:stop, lo], *y_down, keep=keep)

    def y_dir(piece):
        y_near(piece, 1)
        y_near(piece, 3)

    def y_relayed(piece, by, keep=True):
        start, stop, row, rows = Y_PIECES[piece]
        lo, hi = cut(row, rows)
        slots = slice(start, stop)
        sems = y_sems[piece]
        rows, n, to, target = (lo, 0, y_up, y_from_minus) if by == 1 else (hi, 1, y_down, y_from_plus)
        arrive(sems[n], y_relay.at[slots, rows])
        y_sum[slots, rows] = part[slots, by, rows] + y_relay[slots, rows]
        send(sems[4 + n], y_sum.at[slots, rows], target.at[slots, rows], *to, keep=keep)

    def y_b(piece):
        y_relayed(piece, 1)
        y_relayed(piece, 3)

    def y_a_step(piece, first):
        pl.when(in_first[2] == first)(functools.partial(y_far, piece, first))
        for by in (1, 3):
            pl.when(in_first[by] == first)(functools.partial(y_near, piece, by, first))

    def y_b_step(piece, first):
        for by in (1, 3):
            pl.when(in_first[by] == first)(functools.partial(y_relayed, piece, by, first))

    def y_c(piece):
        start, stop, row, rows = Y_PIECES[piece]
        slots = slice(start, stop)
        lo, hi = cut(row, rows)
        sems = y_sems[piece]
        arrive(sems[2], y_from_minus.at[slots, hi])
        arrive(sems[3], y_from_plus.at[slots, lo])
        arrive(sems[4], y_from_minus.at[slots, lo])
        arrive(sems[5], y_from_plus.at[slots, hi])
        every = slice(row, row + rows)
        for slot in range(start, stop):
            total = part[slot, 0, every].astype(F32) + y_from_minus[slot, every].astype(F32)
            total = total + y_from_plus[slot, every].astype(F32)
            ysum[lax.rem(x + X_ORDER[slot] - z + 4, 4), every] = total.astype(BF16)

    def z_far(piece):
        lo, hi = cut(*Z_PIECES[piece])
        sems = z_sems[piece]
        send(sems[0], ysum.at[2, lo], z_relay.at[lo], *z_up)
        send(sems[1], ysum.at[2, hi], z_relay.at[hi], *z_down)

    def z_dir(piece):
        lo, hi = cut(*Z_PIECES[piece])
        sems = z_sems[piece]
        send(sems[2], ysum.at[1, hi], z_from_minus.at[hi], *z_up)
        send(sems[3], ysum.at[3, lo], z_from_plus.at[lo], *z_down)

    def z_b(piece):
        lo, hi = cut(*Z_PIECES[piece])
        sems = z_sems[piece]
        arrive(sems[0], z_relay.at[lo])
        z_sum[lo] = ysum[1, lo] + z_relay[lo]
        send(sems[4], z_sum.at[lo], z_from_minus.at[lo], *z_up)
        arrive(sems[1], z_relay.at[hi])
        z_sum[hi] = ysum[3, hi] + z_relay[hi]
        send(sems[5], z_sum.at[hi], z_from_plus.at[hi], *z_down)

    def z_c(piece):
        row, rows = Z_PIECES[piece]
        lo, hi = cut(row, rows)
        sems = z_sems[piece]
        arrive(sems[2], z_from_minus.at[hi])
        arrive(sems[3], z_from_plus.at[lo])
        arrive(sems[4], z_from_minus.at[lo])
        arrive(sems[5], z_from_plus.at[hi])
        every = slice(row, row + rows)
        total = ysum[0, every].astype(F32) + z_from_minus[every].astype(F32)
        total = total + z_from_plus[every].astype(F32)
        grad[every] = total.astype(BF16)

    def shift(piece):
        row, rows = Z_PIECES[piece]
        every = slice(row, row + rows)
        send(grad_sems[piece], grad.at[every], grad_prev.at[every], next_dp, own)

    x_next, x_prev, x_far = lax.rem(x + 1, 4), lax.rem(x + 3, 4), lax.rem(x + 2, 4)
    n_up = [new_sem() for _ in range(SLICES)]
    n_down = [new_sem() for _ in range(SLICES)]
    n_far = [[new_sem(), new_sem()] for _ in range(SLICES)]

    def give(src, to_dp, to_own):
        n = new_sem()
        send(n, src, src, to_dp, to_own)
        return n

    n_sib_pair, n_sib = {}, [[] for _ in range(SLICES)]

    def take_pair(part_of):
        arrive(n_pair[part_of], block(pair, part_of, my_tokens))
        n_sib_pair[part_of] = give(block(pair, part_of, my_tokens), sibling, own)

    def along_x(part_of):
        mine = block(pair, 0, my_tokens) if part_of == 0 else slab(x, part_of, my_tokens)
        send(n_up[part_of], mine, mine, dp, x_plus)
        send(n_down[part_of], mine, mine, dp, x_minus)

    def take_near(part_of):
        if part_of == 0:
            arrive(n_first_up, block(x_minus, 0, my_tokens))
            arrive(n_first_down, block(x_plus, 0, my_tokens))
        for n, at_x, half, to in ((n_up, x_prev, 0, x_plus), (n_down, x_next, 1, x_minus)):
            if part_of == 0:
                arrive(n[0], block(lax.rem(at_x * 2 + 1 - z_lo, N_OWN), 0, my_tokens))
            else:
                arrive(n[part_of], slab(at_x, part_of, my_tokens))
            onward = slab(at_x, part_of, half_of(my_tokens, half))
            send(n_far[part_of][half], onward, onward, dp, to)
            n_sib[part_of].append((give(slab(at_x, part_of, my_tokens), sibling, own), slab(at_x, part_of, sib_tokens)))

    def take_far(part_of):
        for half in range(2):
            arrive(n_far[part_of][half], slab(x_far, part_of, half_of(my_tokens, half)))
            n = give(slab(x_far, part_of, half_of(my_tokens, half)), sibling, own)
            n_sib[part_of].append((n, slab(x_far, part_of, half_of(sib_tokens, half))))

    def prod_own(part_of):
        arrive(n_own[part_of], block(own, part_of, sib_tokens))
        products_here(own, part_of)

    def prod_pair(part_of):
        arrive(n_sib_pair[part_of], block(pair, part_of, sib_tokens))
        products_here(pair, part_of)

    def prod_near(part_of):
        for n, ref in n_sib[part_of][:2]:
            arrive(n, ref)
        products(part_of, 1, 3)

    def prod_far(part_of):
        for n, ref in n_sib[part_of][2:]:
            arrive(n, ref)
        products(part_of, 3, 4)

    prod_own(0)
    y_a_step(0, True)
    prod_own(1)
    take_pair(0)
    y_a_step(1, True)
    along_x(0)
    prod_pair(0)
    y_a_step(0, False)
    prod_own(2)
    take_pair(1)
    along_x(1)
    y_a_step(2, True)
    prod_pair(1)
    y_a_step(1, False)
    take_pair(2)
    y_b_step(1, True)
    y_b_step(0, False)
    prod_own(3)
    take_near(0)
    prod_pair(2)
    y_b_step(0, True)
    y_a_step(2, False)
    y_a_step(3, True)
    prod_near(0)
    along_x(2)
    y_dir(4)
    take_near(1)
    y_b_step(1, False)
    y_far(4)
    y_c(0)
    take_far(0)
    y_b_step(2, True)
    prod_near(1)
    prod_far(0)
    take_pair(3)
    along_x(3)
    y_dir(5)
    y_far(5)
    take_near(2)
    y_b(4)
    prod_pair(3)
    take_far(1)
    prod_near(2)
    y_a_step(3, False)
    prod_far(1)
    y_b(5)
    y_far(7)
    y_dir(7)
    y_c(4)
    y_b_step(3, True)
    y_c(5)
    take_far(2)
    take_near(3)
    y_far(6)
    prod_far(2)
    y_b_step(2, False)
    y_far(9)
    prod_near(3)
    z_far(0)
    z_far(1)
    y_b(7)
    take_far(3)
    prod_far(3)
    y_dir(6)
    y_b(6)
    y_b_step(3, False)
    y_b(9)
    y_c(1)
    y_c(7)
    z_dir(0)
    y_dir(9)
    z_far(3)
    z_b(1)
    y_far(10)
    z_dir(1)
    y_far(8)
    z_b(0)
    y_c(2)
    z_dir(3)
    y_c(6)
    z_far(2)
    z_b(3)
    y_far(11)
    y_c(9)
    z_far(5)
    z_dir(5)
    y_c(3)
    y_dir(10)
    y_b(10)
    z_c(0)
    z_dir(2)
    y_b(11)
    y_dir(11)
    y_b(8)
    y_dir(8)
    z_b(5)
    z_b(2)
    y_c(10)
    z_far(6)
    z_dir(6)
    shift(0)
    y_c(11)
    z_dir(7)
    z_far(7)
    z_c(5)
    z_b(6)
    y_c(8)
    z_far(4)
    z_b(7)
    z_dir(4)
    z_c(3)
    z_c(1)
    z_b(4)
    z_c(6)
    shift(1)
    z_c(2)
    shift(3)
    shift(5)
    z_c(7)
    shift(7)
    shift(6)
    shift(2)
    z_c(4)
    shift(4)

    load_stale.wait()
    squares = jnp.zeros((1, 1), F32)
    for half in range(2):
        rows = slice(half * HALF, (half + 1) * HALF)
        left_applied[rows, :] = dot(stale_v[0, 0, rows, :], grad[...]).astype(BF16)
        value = dot(left_applied[rows, :], stale_v[0, 1])
        precond[rows, :] = value
        squares = squares + jnp.sum(value * value, keepdims=True)
    keep_precond = pltpu.make_async_copy(precond, precond_out, local_sems.at[0])
    keep_precond.start()

    def spread(store, value, targets):
        store[0] = jnp.broadcast_to(value, (8, 128))
        sems = [new_sem() for _ in targets]
        for i, target in enumerate(targets):
            send(sems[i], store.at[0], store.at[i + 1], *target)
        return sems

    def collect(store, sems):
        for i, n in enumerate(sems):
            arrive(n, store.at[i + 1])
        return jnp.sum(store[...], axis=0)[0:1, 0:1]

    def root(tile, side, slot, keep):
        total = jnp.zeros((1, 1), F32)
        for half in range(2):
            rows = slice(half * HALF, (half + 1) * HALF)
            if side == 0:
                value = dot(tile[rows, :], tile[...], (1, 1))
            else:
                value = dot(tile[:, rows], tile[...], (0, 0))
            value = value + EPSILON * identity_rows(half * HALF, HALF)
            stat[rows, :] = value
            total = total + jnp.sum(value * value, keepdims=True)
        scale = 2.5 / jnp.sqrt(total)
        matrix = stat[...] * scale
        stat[...] = matrix
        stat_b[...] = matrix.astype(BF16)
        for half in range(2):
            rows = slice(half * HALF, (half + 1) * HALF)
            squared = dot(stat_b[rows, :], stat_b[...])
            matrix = stat[rows, :]
            mid_n[rows, :] = (5.0 * matrix - squared) * 0.25
            mid_e[rows, :] = ((squared - 10.0 * matrix) * 0.0625).astype(BF16)
        for half in range(2):
            rows = slice(half * HALF, (half + 1) * HALF)
            value = 1.5625 * mid_n[rows, :] + dot(mid_e[rows, :], mid_n[...].astype(BF16))
            mid_t[rows, :] = value
            mid_tb[rows, :] = value.astype(BF16)
        factor = jnp.sqrt(jnp.sqrt(scale)) * 0.25
        for half in range(2):
            rows = slice(half * HALF, (half + 1) * HALF)
            value = 1.5625 * mid_t[rows, :] + dot(mid_e[rows, :], mid_tb[...])
            first = (25.0 * identity_rows(half * HALF, HALF) - 5.0 * stat[rows, :]) * 0.25
            result = ((first - value) * factor).astype(BF16)
            fresh[slot, side, rows, :] = (result.astype(F32) * keep).astype(BF16)

    keep_fresh = []

    def keep_root(slot, side):
        copy = pltpu.make_async_copy(fresh.at[slot, side], fresh_out.at[slot, side], local_sems.at[4 + 2 * slot + side])
        copy.start()
        keep_fresh.append(copy)

    sems1 = spread(norm1, squares, [(dp, own_at(i)) for i in range(1, N_OWN)])
    keep = 1.0 - flag[0:1, 0:1]
    root(grad, 0, 0, keep)
    keep_root(0, 0)
    sems2 = spread(norm2, collect(norm1, sems1), [(dp_at(i), own) for i in range(1, N_DP)])
    root(grad, 1, 0, keep)
    keep_root(0, 1)
    arrive(n_flag, flag_prev)
    for n, (row, rows) in zip(grad_sems, Z_PIECES):
        arrive(n, grad_prev.at[row:row + rows])
    keep = flag_prev[0:1, 0:1]
    for side in range(2):
        root(grad_prev, side, 1, keep)
        keep_root(1, side)
    norm_out[...] = jnp.broadcast_to(collect(norm2, sems2), (8, 128))

    for copy in keep_fresh:
        copy.wait()
    keep_precond.wait()
    for n, shape in sent:
        if shape[0] == 8:
            ref = norm1.at[0]
        elif len(shape) == 2:
            ref = part.at[0, 0, 0:shape[0], 0:shape[1]]
        else:
            ref = part.at[0:shape[0], 0, 0:shape[1]]
        pltpu.make_async_remote_copy(
            src_ref=ref, dst_ref=ref, send_sem=send_sems.at[n], recv_sem=recv_sems.at[n],
            device_id=(sibling, own), device_id_type=MESH,
        ).wait_send()
    assert counter[0] <= N_SEMS, counter[0]


def finish(precond, fresh, norm, update, fresh_out, value, result, roots, sems):
    tiles = [(slot, side) for slot in range(2) for side in range(2)]
    load = pltpu.make_async_copy(precond, value, sems.at[0])
    loads = [pltpu.make_async_copy(fresh.at[t], roots.at[t], sems.at[2 + i]) for i, t in enumerate(tiles)]
    stores = [pltpu.make_async_copy(roots.at[t], fresh_out.at[t], sems.at[6 + i]) for i, t in enumerate(tiles)]
    store = pltpu.make_async_copy(result, update, sems.at[1])
    load.start()
    for copy in loads:
        copy.start()
    scale = lax.rsqrt(norm[0:1, 0:1] / ENTRIES + 1e-06)
    load.wait()
    result[0] = (value[...] * scale).astype(BF16)
    store.start()
    for arrived, leave in zip(loads, stores):
        arrived.wait()
        leave.start()
    for copy in stores + [store]:
        copy.wait()


def body(activations, out_grads, moved_tiles, stale_roots):
    tile = (BS, BS)
    scratch = [
        ((SLICES, 2 * BS, N_OWN * SLICE), BF16),
        ((2, 2 * BS, BS), BF16),
        ((4, 4) + tile, BF16),
        ((4,) + tile, BF16), ((4,) + tile, BF16), ((4,) + tile, BF16), ((4,) + tile, BF16),
        ((4,) + tile, BF16),
        (tile, BF16), (tile, BF16), (tile, BF16), (tile, BF16),
        (tile, BF16), (tile, BF16), ((8, 128), F32), ((8, 128), F32), ((1, 2) + tile, BF16),
        (tile, BF16), (tile, F32), (tile, F32), (tile, BF16), (tile, F32), (tile, BF16),
        (tile, F32), (tile, BF16),
        ((N_OWN, 8, 128), F32), ((N_DP, 8, 128), F32), ((2, 2) + tile, BF16),
    ]
    flops = 2 * 2 * 512 * 4096 * 2048
    precond, fresh, norm = pl.pallas_call(
        kernel,
        out_shape=(
            jax.ShapeDtypeStruct(tile, F32),
            jax.ShapeDtypeStruct((2, 2) + tile, BF16),
            jax.ShapeDtypeStruct((8, 128), F32),
        ),
        in_specs=[
            pl.BlockSpec(memory_space=pl.ANY),
            pl.BlockSpec(memory_space=pl.ANY),
            pl.BlockSpec(memory_space=pltpu.SMEM),
            pl.BlockSpec(memory_space=pl.ANY),
        ],
        out_specs=(
            pl.BlockSpec(memory_space=pl.ANY),
            pl.BlockSpec(memory_space=pl.ANY),
            pl.BlockSpec(memory_space=pltpu.VMEM),
        ),
        scratch_shapes=[pltpu.VMEM(shape, dtype) for shape, dtype in scratch] + [
            pltpu.SemaphoreType.DMA((N_SEMS,)),
            pltpu.SemaphoreType.DMA((N_SEMS,)),
            pltpu.SemaphoreType.DMA((4 + SLICES,)),
        ],
        compiler_params=pltpu.CompilerParams(
            collective_id=0, has_side_effects=True, vmem_limit_bytes=60 * 1024 * 1024
        ),
        cost_estimate=pl.CostEstimate(flops=flops, bytes_accessed=6 << 20, transcendentals=0),
    )(activations, out_grads, moved_tiles, stale_roots)
    return tuple(pl.pallas_call(
        finish,
        out_shape=(
            jax.ShapeDtypeStruct((1,) + tile, BF16),
            jax.ShapeDtypeStruct((2, 2) + tile, BF16),
        ),
        in_specs=[
            pl.BlockSpec(memory_space=pl.ANY),
            pl.BlockSpec(memory_space=pl.ANY),
            pl.BlockSpec(memory_space=pltpu.VMEM),
        ],
        out_specs=(pl.BlockSpec(memory_space=pl.ANY), pl.BlockSpec(memory_space=pl.ANY)),
        scratch_shapes=[
            pltpu.VMEM(tile, F32),
            pltpu.VMEM((1,) + tile, BF16),
            pltpu.VMEM((2, 2) + tile, BF16),
            pltpu.SemaphoreType.DMA((10,)),
        ],
    )(precond, fresh, norm))


def solution(mesh):
    in_specs = (P("dp", "own"), P("dp", "own"), P("dp", "own"), P("dp", None, None, "own"))
    out_specs = (P("dp", None, "own"), P("dp", None, None, "own"))
    return jax.shard_map(body, mesh=mesh, in_specs=in_specs, out_specs=out_specs, check_vma=False)
```

time: 140 us -> 125 us (0.89)
  Pallas kernels: 134 us -> 123 us
  local copies, waits for them, and re-layouts: 4.91 us -> 0 us
    pallas_call x1 -> x2, Pallas kernels: 134 us -> 123 us  [the longest x1 119 us: body(): pl.pallas_call(kernel, out_shape=(jax.ShapeDtypeStruct(tile, F32), jax.Sh...]
    unnamed x2 -> x0, local copies, waits for them, and re-layouts: 4.91 us -> none
where the time goes in v2:
time: 125 us; the launch traced here: 124 us
  Pallas kernels  123 us (98%)
  between operations  1.44 us (1%)
    pallas_call x1, Pallas kernels, body(): pl.pallas_call(kernel, out_shape=(jax.ShapeDtypeStruct(tile, F32), jax.Sh...  119 us
    pallas_call x1, Pallas kernels, body(): pl.pallas_call(finish, out_shape=(jax.ShapeDtypeStruct((1,) + tile, BF16)...  3.58 us

profile of v2, /device:TPU:1, one launch (start us, length us, event | category | flops | bytes accessed | tf_op | source)
XLA Modules:
  0.0 124.5 jit_solution(5193382391151353586)
XLA Ops:
  1.3 119.4 %shard_map.59 = (f32[512,512]{1,0:T(8,128)}, bf16[2,2,512,512]{3,2,1,0:T(8,128)(2,1)}, f32[8,128]{1,0:T(8,128)}) custom-call(bf16[512,512]{1,0:T(8,128)(2,1)} %act.1, bf16[512,2048]{1,0:T(8,128)(2,1)} %grads.1, s32[1,1]{1,0:T(1,128)S(6)} %copy.6.moved, bf16[1,2,512,512]{3,2,1,0:T(8,128)(2,1)} %stale.1), custom_call_target="tpu_custom_call" | custom-call | flops 17179869184 | bytes 6291456 | tf_op jit(solution)/shard_map/pallas_call | solution.py:616
  120.7 3.6 %shard_map.60 = (bf16[1,512,512]{2,1,0:T(8,128)(2,1)}, bf16[2,2,512,512]{3,2,1,0:T(8,128)(2,1)}) custom-call(f32[512,512]{1,0:T(8,128)} %get-tuple-element.5.precond, bf16[2,2,512,512]{3,2,1,0:T(8,128)(2,1)} %get-tuple-element.6.fresh, f32[8,128]{1,0:T(8,128)} %get-tuple-element.7.norm), custom_call_target="tpu_custom_call" | custom-call | tf_op jit(solution)/shard_map/pallas_call | solution.py:644

commit v3 on v2

--- a/solution.py
+++ b/solution.py
@@ -132,9 +132,12 @@
     load_stale = pltpu.make_async_copy(stale, stale_v, local_sems.at[3])
     load_stale.start()
 
+    cross = lax.rem(dp + 2 * core - 1 + N_DP, N_DP)
     barrier = pltpu.get_barrier_semaphore()
     partners = [(dp, own_at(i)) for i in range(1, 8)]
-    partners += [(dp_at(i), own) for i in range(1, N_DP)]
+    partners += [(sibling, own_at(i)) for i in range(N_OWN)]
+    partners += [(dp_at(2 * i), own) for i in range(1, N_DP // 2)]
+    partners += [(cross, own)]
     for partner in partners:
         pl.semaphore_signal(barrier, inc=1, device_id=partner, device_id_type=MESH)
 
@@ -545,11 +548,12 @@
         copy.start()
         keep_fresh.append(copy)
 
-    sems1 = spread(norm1, squares, [(dp, own_at(i)) for i in range(1, N_OWN)])
+    near = [(dp, own_at(i)) for i in range(1, N_OWN)] + [(sibling, own_at(i)) for i in range(N_OWN)]
+    sems1 = spread(norm1, squares, near)
     keep = 1.0 - flag[0:1, 0:1]
     root(grad, 0, 0, keep)
     keep_root(0, 0)
-    sems2 = spread(norm2, collect(norm1, sems1), [(dp_at(i), own) for i in range(1, N_DP)])
+    sems2 = spread(norm2, collect(norm1, sems1), [(dp_at(2 * i), own) for i in range(1, N_DP // 2)])
     root(grad, 1, 0, keep)
     keep_root(0, 1)
     arrive(n_flag, flag_prev)
@@ -580,21 +584,22 @@
 
 def finish(precond, fresh, norm, update, fresh_out, value, result, roots, sems):
     tiles = [(slot, side) for slot in range(2) for side in range(2)]
-    load = pltpu.make_async_copy(precond, value, sems.at[0])
-    loads = [pltpu.make_async_copy(fresh.at[t], roots.at[t], sems.at[2 + i]) for i, t in enumerate(tiles)]
-    stores = [pltpu.make_async_copy(roots.at[t], fresh_out.at[t], sems.at[6 + i]) for i, t in enumerate(tiles)]
-    store = pltpu.make_async_copy(result, update, sems.at[1])
-    load.start()
-    for copy in loads:
+    halves = [slice(half * HALF, (half + 1) * HALF) for half in range(2)]
+    loads = [pltpu.make_async_copy(fresh.at[t], roots.at[t], sems.at[i]) for i, t in enumerate(tiles)]
+    stores = [pltpu.make_async_copy(roots.at[t], fresh_out.at[t], sems.at[4 + i]) for i, t in enumerate(tiles)]
+    values = [pltpu.make_async_copy(precond.at[h], value.at[h], sems.at[8 + i]) for i, h in enumerate(halves)]
+    results = [pltpu.make_async_copy(result.at[0, h], update.at[0, h], sems.at[10 + i]) for i, h in enumerate(halves)]
+    for copy in loads + values:
         copy.start()
     scale = lax.rsqrt(norm[0:1, 0:1] / ENTRIES + 1e-06)
-    load.wait()
-    result[0] = (value[...] * scale).astype(BF16)
-    store.start()
     for arrived, leave in zip(loads, stores):
         arrived.wait()
         leave.start()
-    for copy in stores + [store]:
+    for rows, arrived, leave in zip(halves, values, results):
+        arrived.wait()
+        result[0, rows] = (value[rows] * scale).astype(BF16)
+        leave.start()
+    for copy in stores + results:
         copy.wait()
 
 
@@ -610,7 +615,7 @@
         (tile, BF16), (tile, BF16), ((8, 128), F32), ((8, 128), F32), ((1, 2) + tile, BF16),
         (tile, BF16), (tile, F32), (tile, F32), (tile, BF16), (tile, F32), (tile, BF16),
         (tile, F32), (tile, BF16),
-        ((N_OWN, 8, 128), F32), ((N_DP, 8, 128), F32), ((2, 2) + tile, BF16),
+        ((2 * N_OWN, 8, 128), F32), ((N_DP // 2, 8, 128), F32), ((2, 2) + tile, BF16),
     ]
     flops = 2 * 2 * 512 * 4096 * 2048
     precond, fresh, norm = pl.pallas_call(
@@ -657,7 +662,7 @@
             pltpu.VMEM(tile, F32),
             pltpu.VMEM((1,) + tile, BF16),
             pltpu.VMEM((2, 2) + tile, BF16),
-            pltpu.SemaphoreType.DMA((10,)),
+            pltpu.SemaphoreType.DMA((12,)),
         ],
     )(precond, fresh, norm))
 

time: 125 us -> 124 us (level)
  no operation moved by 1% of the time
where the time goes in v3:
time: 124 us
  Pallas kernels  122 us (98%)
  between operations  1.44 us (1%)
    pallas_call x1, Pallas kernels, body(): pl.pallas_call(kernel, out_shape=(jax.ShapeDtypeStruct(tile, F32), jax.Sh...  119 us
    pallas_call x1, Pallas kernels, body(): pl.pallas_call(finish, out_shape=(jax.ShapeDtypeStruct((1,) + tile, BF16)...  3.34 us

profile of v3, /device:TPU:1, one launch (start us, length us, event | category | flops | bytes accessed | tf_op | source)
XLA Modules:
  0.0 123.8 jit_solution(18132369733402088339)
XLA Ops:
  1.3 119.0 %shard_map.59 = (f32[512,512]{1,0:T(8,128)}, bf16[2,2,512,512]{3,2,1,0:T(8,128)(2,1)}, f32[8,128]{1,0:T(8,128)}) custom-call(bf16[512,512]{1,0:T(8,128)(2,1)} %act.1, bf16[512,2048]{1,0:T(8,128)(2,1)} %grads.1, s32[1,1]{1,0:T(1,128)S(6)} %copy.6.moved, bf16[1,2,512,512]{3,2,1,0:T(8,128)(2,1)} %stale.1), custom_call_target="tpu_custom_call" | custom-call | flops 17179869184 | bytes 6291456 | tf_op jit(solution)/shard_map/pallas_call | solution.py:621
  120.3 3.3 %shard_map.60 = (bf16[1,512,512]{2,1,0:T(8,128)(2,1)}, bf16[2,2,512,512]{3,2,1,0:T(8,128)(2,1)}) custom-call(f32[512,512]{1,0:T(8,128)} %get-tuple-element.5.precond, bf16[2,2,512,512]{3,2,1,0:T(8,128)(2,1)} %get-tuple-element.6.fresh, f32[8,128]{1,0:T(8,128)} %get-tuple-element.7.norm), custom_call_target="tpu_custom_call" | custom-call | tf_op jit(solution)/shard_map/pallas_call | solution.py:649

commit v4 on v3

--- a/solution.py
+++ b/solution.py
@@ -519,25 +519,25 @@
             stat[rows, :] = value
             total = total + jnp.sum(value * value, keepdims=True)
         scale = 2.5 / jnp.sqrt(total)
-        matrix = stat[...] * scale
-        stat[...] = matrix
-        stat_b[...] = matrix.astype(BF16)
+        stat_b[...] = (stat[...] * scale).astype(BF16)
         for half in range(2):
             rows = slice(half * HALF, (half + 1) * HALF)
             squared = dot(stat_b[rows, :], stat_b[...])
-            matrix = stat[rows, :]
-            mid_n[rows, :] = (5.0 * matrix - squared) * 0.25
+            matrix = stat[rows, :] * scale
+            value = (5.0 * matrix - squared) * 0.25
+            mid_n[rows, :] = value
+            left_applied[rows, :] = value.astype(BF16)
             mid_e[rows, :] = ((squared - 10.0 * matrix) * 0.0625).astype(BF16)
         for half in range(2):
             rows = slice(half * HALF, (half + 1) * HALF)
-            value = 1.5625 * mid_n[rows, :] + dot(mid_e[rows, :], mid_n[...].astype(BF16))
+            value = 1.5625 * mid_n[rows, :] + dot(mid_e[rows, :], left_applied[...])
             mid_t[rows, :] = value
             mid_tb[rows, :] = value.astype(BF16)
         factor = jnp.sqrt(jnp.sqrt(scale)) * 0.25
         for half in range(2):
             rows = slice(half * HALF, (half + 1) * HALF)
             value = 1.5625 * mid_t[rows, :] + dot(mid_e[rows, :], mid_tb[...])
-            first = (25.0 * identity_rows(half * HALF, HALF) - 5.0 * stat[rows, :]) * 0.25
+            first = (25.0 * identity_rows(half * HALF, HALF) - 5.0 * (stat[rows, :] * scale)) * 0.25
             result = ((first - value) * factor).astype(BF16)
             fresh[slot, side, rows, :] = (result.astype(F32) * keep).astype(BF16)
 

time: 124 us -> 124 us (level)
  no operation moved by 1% of the time
where the time goes in v4:
time: 124 us
  Pallas kernels  122 us (98%)
  between operations  1.44 us (1%)
    pallas_call x1, Pallas kernels, body(): pl.pallas_call(kernel, out_shape=(jax.ShapeDtypeStruct(tile, F32), jax.Sh...  119 us
    pallas_call x1, Pallas kernels, body(): pl.pallas_call(finish, out_shape=(jax.ShapeDtypeStruct((1,) + tile, BF16)...  3.34 us

profile of v4, /device:TPU:1, one launch (start us, length us, event | category | flops | bytes accessed | tf_op | source)
XLA Modules:
  0.0 123.8 jit_solution(18132369733402088339)
XLA Ops:
  1.3 119.0 %shard_map.59 = (f32[512,512]{1,0:T(8,128)}, bf16[2,2,512,512]{3,2,1,0:T(8,128)(2,1)}, f32[8,128]{1,0:T(8,128)}) custom-call(bf16[512,512]{1,0:T(8,128)(2,1)} %act.1, bf16[512,2048]{1,0:T(8,128)(2,1)} %grads.1, s32[1,1]{1,0:T(1,128)S(6)} %copy.6.moved, bf16[1,2,512,512]{3,2,1,0:T(8,128)(2,1)} %stale.1), custom_call_target="tpu_custom_call" | custom-call | flops 17179869184 | bytes 6291456 | tf_op jit(solution)/shard_map/pallas_call | solution.py:621
  120.3 3.3 %shard_map.60 = (bf16[1,512,512]{2,1,0:T(8,128)(2,1)}, bf16[2,2,512,512]{3,2,1,0:T(8,128)(2,1)}) custom-call(f32[512,512]{1,0:T(8,128)} %get-tuple-element.5.precond, bf16[2,2,512,512]{3,2,1,0:T(8,128)(2,1)} %get-tuple-element.6.fresh, f32[8,128]{1,0:T(8,128)} %get-tuple-element.7.norm), custom_call_target="tpu_custom_call" | custom-call | tf_op jit(solution)/shard_map/pallas_call | solution.py:649
